TPU v7x, 512 devices: a whole 4x4x16 slice. The times are simulated.
512 devices in a mesh: rows: 16 (over z_hi, x, core), labels: 32 (over y, z_lo).
Axes of the slice: x: 4, y: 4, z: 16 (z_hi: 2, z_lo: 8; z = z_hi * 8 + z_lo), core: 2. Of those that a mesh axis runs over, the one named last changes fastest.
Arguments:
- pool_features: bfloat16 [2048, 768], P('rows'), may hold values from -6 to 6
- pool_labels: int32 [2048, 16], P('rows'), may hold values from 0 to 196607
- pool_counts: int32 [2048], P('rows'), may hold values from 1 to 16
- batch_rows: int32 [2, 512], P(None, 'rows'), may hold values from 0 to 127
- weights: float32 [196608, 768], P(('rows', 'labels')), may hold values from -0.21875 to 0.21875
- momentum: float32 [196608, 768], P(('rows', 'labels')), may hold values from -24 to 24
Outputs:
- new_weights: float32 [196608, 768], P(('rows', 'labels'))
- new_momentum: float32 [196608, 768], P(('rows', 'labels'))
- feature_grads: float32 [2, 512, 768], P(None, 'rows')
Inputs may be any that keep to these rules, and one draw needn't show every extreme that they name: `pool_labels`: slots of a list at or past its count are padding and are ignored; a label may appear twice in a list. `batch_rows`: an entry names one of the 128 examples stored with the index of rows that owns that batch row.
All inputs are finite; a program needn't handle non-finite values.
Results may differ from a plain program's by a relative error of at most 0.00045.
The roundings to bfloat16 on the way count: a program that leaves them out, or rounds other values in their place, can miss the bound.
Values may be sent and summed in bfloat16 or wider, within the bound.
A program may use at most 64 MiB of HBM per device.

v0:
```python
import math
import jax
import jax.numpy as jnp
from jax import lax
from jax.sharding import PartitionSpec as P

learn_rate = 0.001
decay_rate = 0.9


def side_by_side(arrays, axis, dim, along):
    widths = [math.prod(a.shape[along:]) for a in arrays]
    both = jnp.concatenate(
        [a.reshape(*a.shape[:along], w) for a, w in zip(arrays, widths)], axis=along
    )
    filled = lax.all_gather(both, axis, axis=dim, tiled=True)
    tiles = jnp.split(filled, [sum(widths[:k]) for k in range(1, len(widths))], axis=along)
    return tuple(
        (b.reshape(*filled.shape[:along], *a.shape[along:]) for a, b in zip(arrays, tiles))
    )


def feature_sums(errors_list, lowered_list, group_rows, width):
    parts = []
    for errors, low_weights in zip(errors_list, lowered_list):
        parts.append(jnp.dot(errors, low_weights, preferred_element_type=jnp.float32))
    whole = lax.psum(jnp.concatenate(parts, axis=1), ("rows", "labels"))
    mine = lax.dynamic_slice_in_dim(whole, lax.axis_index("rows") * group_rows, group_rows, 0)
    return jnp.stack([mine[:, :width], mine[:, width:]])


def per_device(pool_features, pool_labels, pool_counts, batch_rows, weights, momentum):
    lab_rows = weights.shape[0]
    group_rows = batch_rows.shape[1]
    width = weights.shape[1]
    device_index = lax.axis_index("rows") * lax.axis_size("labels") + lax.axis_index("labels")
    labels = device_index * lab_rows + jnp.arange(lab_rows, dtype=jnp.int32)
    all_ids, all_counts = side_by_side(
        (pool_labels[batch_rows], pool_counts[batch_rows]), "rows", 1, 2
    )
    all_features = lax.all_gather(pool_features[batch_rows], "rows", axis=1, tiled=True)
    errors_list = []
    lowered_list = []
    for batch in range(2):
        features = all_features[batch]
        label_ids = all_ids[batch]
        in_list = (
            jnp.arange(label_ids.shape[1], dtype=jnp.int32)[None, :] < all_counts[batch][:, None]
        )
        matched = (label_ids[:, :, None] == labels[None, None, :]) & in_list[:, :, None]
        targets = jnp.any(matched, axis=1).astype(jnp.float32)
        low_weights = weights.astype(jnp.bfloat16)
        logits = lax.dot_general(
            features, low_weights, (((1,), (1,)), ((), ())), preferred_element_type=jnp.float32
        )
        errors = (jax.nn.sigmoid(logits) - targets).astype(jnp.bfloat16)
        grads = lax.dot_general(
            errors, features, (((0,), (0,)), ((), ())), preferred_element_type=jnp.float32
        )
        errors_list.append(errors)
        lowered_list.append(low_weights)
        momentum = decay_rate * momentum + grads
        weights = weights - learn_rate * momentum
    return (weights, momentum, feature_sums(errors_list, lowered_list, group_rows, width))


def solution(mesh):
    in_specs = (
        P("rows", None),
        P("rows", None),
        P("rows"),
        P(None, "rows"),
        P(("rows", "labels"), None),
        P(("rows", "labels"), None),
    )
    out_specs = (P(("rows", "labels"), None), P(("rows", "labels"), None), P(None, "rows", None))
    return jax.shard_map(
        per_device, mesh=mesh, in_specs=in_specs, out_specs=out_specs, check_vma=False
    )
```

profile of v0, /device:TPU:2, one launch (start us, length us, event | category | flops | bytes accessed | tf_op | source)
XLA Modules:
  0.0 595.8 jit_solution(10529048860126078827)
XLA Ops:
  7.2 0.0 copy-start
  7.2 0.0 copy-start.1
  7.2 0.0 copy-start.5
  7.2 0.0 all-gather.3.cloned.1.call-start
  7.2 0.7 compare_select_fusion
  8.0 0.1 reshape.71
  8.1 0.0 copy-done
  8.1 1.3 gather_fusion
  9.4 0.0 all-gather.3.cloned.1.call-update
  9.5 0.0 all-reduce.2.cloned.1.call-start
  9.5 0.0 copy-done.1
  9.5 0.8 gather_fusion.2
  10.3 0.1 reshape.68
  10.4 0.1 copy.21
  10.5 0.0 copy-done.5
  10.5 0.1 copy.19
  10.6 0.6 gather_fusion.1
  11.2 0.1 pad_add_fusion
  11.4 0.0 copy-start.2
  11.4 46.1 %all_gather.7 = s32[2,512,17]{2,0,1:T(2,128)S(1)} all-gather(s32[2,32,17]{2,0,1:T(2,128)S(1)} %pad_add_fusion), channel_id=1, replica_groups=mesh['rows'=16,'labels'=32] {'rows'}, dimensions={1}, use_global_device_ids=true | all-gather | bytes 73984 | tf_op jit(solution)/shard_map/all_gather | solution.py:16
  57.4 19.6 %slice_reduce_fusion = (s32[512]{0:T(512)S(1)}, s32[512]{0:T(512)S(1)}) fusion(s32[2,512,17]{2,0,1:T(2,128)S(1)} %all_gather.7), kind=kLoop, calls=%fused_computation.28 | loop fusion | bytes 8192 | tf_op jit(solution)/shard_map/slice | solution.py:48
  77.1 0.2 iota_compare_fusion
  77.3 0.4 fusion.14
  77.7 8.2 %and_reduce_fusion = (pred[512,384]{1,0:T(8,128)(4,1)S(1)}, pred[512,384]{1,0:T(8,128)(4,1)S(1)}) fusion(s32[512,16]{1,0:T(8,128)S(1)} %bitcast.27, s32[384]{0:T(512)S(1)} %iota_add_fusion, pred[512,16]{1,0:T(8,128)(4,1)S(1)} %get-tuple-element.15, pred[512,16]{1,0:T(8,128)(4,1)S(1)} %get-tuple-element.16, s32[512,16]{1,0:T(8,128)S(1)} %bitcast.26), kind=kLoop, calls=%fused_computation.3 | loop fusion | flops 18481152 | bytes 476672 | tf_op jit(solution)/shard_map/reduce_or | solution.py:51
  85.9 17.5 %all-gather.3.cloned.1.call-done = bf16[2,512,768]{2,1,0:T(8,128)(2,1)} async-done(((bf16[2,32,768]{2,1,0:T(8,128)(2,1)}), bf16[2,512,768]{2,1,0:T(8,128)(2,1)}) %all-gather.3.cloned.1.call-update) | async-done | bytes 1572880 | tf_op jit(solution)/shard_map/all_gather | solution.py:41
  103.4 0.0 copy-done.2
  103.4 1.8 fusion.9
  105.2 0.0 copy-start.3
  105.2 0.0 copy-start.4
  105.2 0.6 fusion.11
  105.8 0.8 copy-done.3
  106.6 0.3 copy-done.4
  106.9 0.6 fusion.10
  107.5 0.7 fusion.8
  108.1 0.6 fusion.15
  108.7 2.1 pad_maximum_fusion
  110.8 0.0 all-reduce.2.cloned.1.call-update
  110.8 3.2 multiply_subtract_fusion
  113.9 473.3 %all-reduce.2.cloned.1.call-done = f32[512,1536]{1,0:T(8,128)} async-done(((f32[512,1536]{1,0:T(8,128)}), f32[512,1536]{1,0:T(8,128)}) %all-reduce.2.cloned.1.call-update) | async-done | bytes 3145744 | tf_op jit(solution)/shard_map/psum | solution.py:27
  587.3 1.0 dynamic-slice_bitcast_fusion.1
  588.2 0.7 pad_maximum_fusion.1
  (3 shorter events, 0.0 us)
Async XLA Ops:
  7.2 0.9 copy-start
  7.2 2.3 copy-start.1
  7.2 3.3 copy-start.5
  7.2 96.2 %all-gather.3.cloned.1.call-start = ((), (), s32[]{:S(2)}) async-start(), calls=%async_computation.1 | async-start | bytes 1671168 | tf_op jit(solution)/shard_map/all_gather | solution.py:41
  9.5 577.8 %all-reduce.2.cloned.1.call-start = ((), (), s32[]{:S(2)}) async-start(), calls=%async_computation | async-start | bytes 6291456 | tf_op jit(solution)/shard_map/psum | solution.py:27
  11.4 92.0 %copy-start.2 = (f32[384,768]{1,0:T(8,128)S(1)}, f32[384,768]{1,0:T(8,128)}, u32[]{:S(2)}) copy-start(f32[384,768]{1,0:T(8,128)} %param.10) | copy-start | bytes 3538948
  105.2 1.4 copy-start.3
  105.2 1.7 copy-start.4
Sparse Core Ops, SparseCore 0:
  12.0 91.3 all-gather.2
  110.9 476.3 all-reduce.1
where the time goes:
time: 596 us
  waiting for transfers between devices  491 us (82%)
  blocking collectives  46.1 us (8%)
  local copies, waits for them, and re-layouts  25.3 us (4%)
  between operations  14.2 us (2%)
  other arithmetic  12 us (2%)
  matrix products  7.3 us (1%)
    psum x1, waiting for transfers between devices, feature_sums(): whole = lax.psum(jnp.concatenate(parts, axis=1), ('rows', 'labels'))  473 us
    all_gather x1, blocking collectives, side_by_side(): filled = lax.all_gather(both, axis, axis=dim, tiled=True)  46.1 us
    slice x1, local copies, waits for them, and re-layouts, per_device(): all_counts[batch][:, None]  19.6 us
    all_gather x1, waiting for transfers between devices, per_device(): lax.all_gather(pool_features[batch_rows], 'rows', axis=1, tiled=True)  17.5 us
  transfers between devices with their start and end apart: 2, of which 2 were waited for; matrix products, arithmetic and copies ran while one was open for 6% of the time, Pallas kernels for 0%

commit v1 on v0

--- a/solution.py
+++ b/solution.py
@@ -24,7 +24,7 @@
     parts = []
     for errors, low_weights in zip(errors_list, lowered_list):
         parts.append(jnp.dot(errors, low_weights, preferred_element_type=jnp.float32))
-    whole = lax.psum(jnp.concatenate(parts, axis=1), ("rows", "labels"))
+    whole = lax.psum(lax.psum(jnp.concatenate(parts, axis=1), "rows"), "labels")
     mine = lax.dynamic_slice_in_dim(whole, lax.axis_index("rows") * group_rows, group_rows, 0)
     return jnp.stack([mine[:, :width], mine[:, width:]])
 

time: 596 us -> 882 us (1.48)
  the two profiles are of different devices: /device:TPU:2 before, /device:TPU:34 now
where the time goes in v1:
time: 882 us
  waiting for transfers between devices  783 us (89%)
  blocking collectives  40.8 us (5%)
  local copies, waits for them, and re-layouts  25.3 us (3%)
  between operations  13.9 us (2%)
  other arithmetic  12 us (1%)
    psum x2, waiting for transfers between devices, feature_sums(): whole = lax.psum(lax.psum(jnp.concatenate(parts, axis=1), 'rows'), 'labels')  766 us
    all_gather x1, blocking collectives, side_by_side(): filled = lax.all_gather(both, axis, axis=dim, tiled=True)  40.8 us
    slice x1, local copies, waits for them, and re-layouts, per_device(): all_counts[batch][:, None]  19.6 us
  transfers between devices with their start and end apart: 3, of which 3 were waited for; matrix products, arithmetic and copies ran while one was open for 4% of the time, Pallas kernels for 0%

profile of v1, /device:TPU:34, one launch (start us, length us, event | category | flops | bytes accessed | tf_op | source)
XLA Modules:
  0.0 882.1 jit_solution(3548688595397934338)
XLA Ops:
  7.2 0.0 copy-start
  7.2 0.0 copy-start.1
  7.2 0.0 copy-start.5
  7.2 0.0 all-gather.3.cloned.1.call-start
  7.2 0.7 compare_select_fusion
  8.0 0.1 reshape.71
  8.1 0.0 copy-done
  8.1 1.3 gather_fusion
  9.4 0.0 all-gather.3.cloned.1.call-update
  9.5 0.0 all-reduce.3.cloned.1.call-start
  9.5 0.0 copy-done.1
  9.5 0.8 gather_fusion.2
  10.3 0.1 reshape.68
  10.4 0.1 copy.21
  10.5 0.0 copy-done.5
  10.5 0.1 copy.19
  10.6 0.6 gather_fusion.1
  11.2 0.1 pad_add_fusion
  11.4 0.0 copy-start.2
  11.4 40.8 %all_gather.7 = s32[2,512,17]{2,0,1:T(2,128)S(1)} all-gather(s32[2,32,17]{2,0,1:T(2,128)S(1)} %pad_add_fusion), channel_id=1, replica_groups=mesh['rows'=16,'labels'=32] {'rows'}, dimensions={1}, use_global_device_ids=true | all-gather | bytes 73984 | tf_op jit(solution)/shard_map/all_gather | solution.py:16
  52.2 19.6 %slice_reduce_fusion = (s32[512]{0:T(512)S(1)}, s32[512]{0:T(512)S(1)}) fusion(s32[2,512,17]{2,0,1:T(2,128)S(1)} %all_gather.7), kind=kLoop, calls=%fused_computation.28 | loop fusion | bytes 8192 | tf_op jit(solution)/shard_map/slice | solution.py:48
  71.8 0.2 iota_compare_fusion
  72.0 0.4 fusion.14
  72.4 8.2 and_reduce_fusion
  80.6 17.1 %all-gather.3.cloned.1.call-done = bf16[2,512,768]{2,1,0:T(8,128)(2,1)} async-done(((bf16[2,32,768]{2,1,0:T(8,128)(2,1)}), bf16[2,512,768]{2,1,0:T(8,128)(2,1)}) %all-gather.3.cloned.1.call-update) | async-done | bytes 1572880 | tf_op jit(solution)/shard_map/all_gather | solution.py:41
  97.7 0.0 copy-done.2
  97.7 1.8 fusion.9
  99.5 0.0 copy-start.3
  99.6 0.0 copy-start.4
  99.6 0.6 fusion.11
  100.1 0.8 copy-done.3
  101.0 0.3 copy-done.4
  101.3 0.6 fusion.10
  101.9 0.7 fusion.8
  102.5 0.6 fusion.15
  103.1 2.1 pad_maximum_fusion
  105.1 0.0 all-reduce.3.cloned.1.call-update
  105.2 0.0 all-reduce.5.cloned.1.call-start
  105.2 283.0 %all-reduce.3.cloned.1.call-done = f32[512,1536]{1,0:T(8,128)} async-done(((f32[512,1536]{1,0:T(8,128)}), f32[512,1536]{1,0:T(8,128)}) %all-reduce.3.cloned.1.call-update) | async-done | bytes 3145744 | tf_op jit(solution)/shard_map/psum | solution.py:27
  388.2 0.0 all-reduce.5.cloned.1.call-update
  388.2 3.2 multiply_subtract_fusion
  391.4 482.5 %all-reduce.5.cloned.1.call-done = f32[512,1536]{1,0:T(8,128)} async-done(((f32[512,1536]{1,0:T(8,128)}), f32[512,1536]{1,0:T(8,128)}) %all-reduce.5.cloned.1.call-update) | async-done | bytes 3145744 | tf_op jit(solution)/shard_map/psum | solution.py:27
  873.9 1.0 dynamic-slice_bitcast_fusion.1
  874.9 0.7 pad_maximum_fusion.1
  (3 shorter events, 0.0 us)
Async XLA Ops:
  7.2 0.9 copy-start
  7.2 2.3 copy-start.1
  7.2 3.3 copy-start.5
  7.2 90.5 %all-gather.3.cloned.1.call-start = ((), (), s32[]{:S(2)}) async-start(), calls=%async_computation.2 | async-start | bytes 1671168 | tf_op jit(solution)/shard_map/all_gather | solution.py:41
  9.5 378.7 %all-reduce.3.cloned.1.call-start = ((), (), s32[]{:S(2)}) async-start(), calls=%async_computation | async-start | bytes 6291456 | tf_op jit(solution)/shard_map/psum | solution.py:27
  11.4 86.4 %copy-start.2 = (f32[384,768]{1,0:T(8,128)S(1)}, f32[384,768]{1,0:T(8,128)}, u32[]{:S(2)}) copy-start(f32[384,768]{1,0:T(8,128)} %param.10) | copy-start | bytes 3538948
  99.5 1.4 copy-start.3
  99.6 1.7 copy-start.4
  105.2 768.7 %all-reduce.5.cloned.1.call-start = ((), (), s32[]{:S(2)}) async-start(), calls=%async_computation.1 | async-start | bytes 6291456 | tf_op jit(solution)/shard_map/psum | solution.py:27
Sparse Core Ops, SparseCore 0:
  12.0 85.7 all-gather.2
  105.3 282.8 all-reduce.2
  391.1 482.7 all-reduce.4
